TPU v7x, 32 devices: a whole 2x2x4 slice. The times are simulated.
32 devices in a mesh: blk: 16 (over z, y, x), mp: 2 (over core).
Axes of the slice: x: 2, y: 2, z: 4, core: 2. Of those that a mesh axis runs over, the one named last changes fastest.
Arguments:
- queries: bfloat16 [4096, 5120], P('blk', 'mp'), may hold values from -8.5 to 8.5
- suffix_key_rows: bfloat16 [4096, 1024], P('blk', 'mp'), may hold values from -6 to 6
- suffix_value_rows: bfloat16 [4096, 1024], P('blk', 'mp'), may hold values from -6 to 6
- shared_prefix_keys: bfloat16 [512, 1024], P('blk', 'mp'), may hold values from -8.5 to 8.5
- shared_prefix_values: bfloat16 [512, 1024], P('blk', 'mp'), may hold values from -6 to 6
- out_weight: bfloat16 [5120, 5120], P('mp', 'blk'), may hold values from -0.078125 to 0.078125
- lengths: int32 [16], replicated, may hold values from 1 to 1024, 4096 in all
Outputs:
- output: bfloat16 [4096, 5120], P('blk', 'mp')
Inputs may be any that keep to these rules, and one draw needn't show every extreme that they name: The lengths sum to 4096; the longest is exactly 1024.
All inputs are finite; a program needn't handle non-finite values.
Results may differ from a plain program's by a relative error of at most 0.019.
Values may be sent and summed in bfloat16 or wider, within the bound.
A program may use at most 64 MiB of HBM per device.

v0:
```python
import math

import jax
import jax.numpy as jnp
from jax import lax
from jax.sharding import PartitionSpec as P

HEAD_SIZE = 128


MASKED_SCORE = -1e30


def passed_along(block, axis, distance):
    devices = range(lax.axis_size(axis))
    route = [(i - distance, i) for i in devices if i - distance in devices]
    return lax.ppermute(block, axis, route)


def per_device(
    queries,
    suffix_key_rows,
    suffix_value_rows,
    shared_prefix_keys,
    shared_prefix_values,
    out_weight,
    lengths,
):
    tok_rows = queries.shape[0]
    kv_heads = suffix_key_rows.shape[1] // HEAD_SIZE
    q_heads = queries.shape[1] // HEAD_SIZE
    heads_per_group = q_heads // kv_heads
    blocks = lax.axis_size("blk")
    cycle_reach = blocks // 4
    my_block = lax.axis_index("blk")
    score_scale = 1.0 / math.sqrt(HEAD_SIZE)
    heads_of_query = queries.reshape(tok_rows, kv_heads, heads_per_group, HEAD_SIZE)
    req_ends = jnp.cumsum(lengths)
    local_rows = jnp.arange(tok_rows, dtype=jnp.int32)
    query_pos = my_block * tok_rows + local_rows

    def owner_of(position):
        return jnp.sum((position[:, None] >= req_ends[None, :]).astype(jnp.int32), axis=1)

    query_owner = owner_of(query_pos)

    def update(carry_state, key_block, value_block, visible):
        run_max, row_total, accumulated = carry_state
        count = key_block.shape[0]
        key_heads = key_block.reshape(count, kv_heads, HEAD_SIZE)
        value_heads = value_block.reshape(count, kv_heads, HEAD_SIZE)
        scores = (
            jnp.einsum(
                "qhgd,khd->hgqk", heads_of_query, key_heads, preferred_element_type=jnp.float32
            )
            * score_scale
        )
        if visible is not None:
            scores = jnp.where(visible[None, None], scores, MASKED_SCORE)
        new_max = jnp.maximum(run_max, jnp.max(scores, axis=-1))
        weights = jnp.exp(scores - new_max[..., None])
        if visible is not None:
            weights = jnp.where(visible[None, None], weights, 0.0)
        rescale = jnp.exp(run_max - new_max)
        row_total = row_total * rescale + jnp.sum(weights, axis=-1)
        contrib = jnp.einsum(
            "hgqk,khd->hgqd",
            weights.astype(jnp.bfloat16),
            value_heads,
            preferred_element_type=jnp.float32,
        )
        accumulated = accumulated * rescale[..., None] + contrib
        return (new_max, row_total, accumulated)

    start_state = (
        jnp.full((kv_heads, heads_per_group, tok_rows), MASKED_SCORE, jnp.float32),
        jnp.zeros((kv_heads, heads_per_group, tok_rows), jnp.float32),
        jnp.zeros((kv_heads, heads_per_group, tok_rows, HEAD_SIZE), jnp.float32),
    )
    carry_state = update(
        start_state,
        lax.all_gather(shared_prefix_keys, "blk", axis=0, tiled=True),
        lax.all_gather(shared_prefix_values, "blk", axis=0, tiled=True),
        None,
    )

    def visible_from(distance):
        key_pos = (my_block - distance) * tok_rows + local_rows
        key_owner = owner_of(key_pos)
        return (
            (key_owner[None, :] == query_owner[:, None])
            & (key_pos[None, :] <= query_pos[:, None])
            & (key_pos[None, :] >= 0)
        )

    kv_pair = jnp.stack((suffix_key_rows, suffix_value_rows))
    carry_state = update(carry_state, kv_pair[0], kv_pair[1], visible_from(0))

    def advance(distance, loop_carry):
        current, moving = loop_carry
        moving = passed_along(moving, "blk", 1)
        visible = visible_from(distance)
        current = update(current, moving[0], moving[1], visible)
        return (current, moving)

    carry_state, kv_pair = lax.fori_loop(1, cycle_reach + 1, advance, (carry_state, kv_pair))
    run_max, row_total, accumulated = carry_state
    attended = accumulated / row_total[..., None]
    attn = (
        jnp.transpose(attended, (2, 0, 1, 3))
        .reshape(tok_rows, q_heads * HEAD_SIZE)
        .astype(jnp.bfloat16)
    )
    product = jnp.dot(
        attn,
        lax.all_gather(out_weight, "blk", axis=1, tiled=True),
        preferred_element_type=jnp.float32,
    )
    return lax.psum_scatter(product.astype(jnp.bfloat16), "mp", scatter_dimension=1, tiled=True)


def solution(mesh):
    placed = (
        P("blk", "mp"),
        P("blk", "mp"),
        P("blk", "mp"),
        P("blk", "mp"),
        P("blk", "mp"),
        P("mp", "blk"),
        P(),
    )
    return jax.shard_map(
        per_device, mesh=mesh, in_specs=placed, out_specs=P("blk", "mp"), check_vma=False
    )
```

profile of v0, /device:TPU:5, one launch (start us, length us, event | category | flops | bytes accessed | tf_op | source)
XLA Modules:
  0.0 375.6 jit_solution(9957923385299517175)
XLA Ops:
  6.5 0.7 all-gather.2.cloned.1.call-update
  7.3 1.7 reshape_squeeze_stack.6
  9.0 1.1 copy.67
  10.1 1.7 reshape_squeeze_stack.7
  11.9 1.8 copy.68
  13.7 0.7 copy.59
  14.5 1.6 copy.56
  16.2 37.9 %all_gather.9 = bf16[512,512]{1,0:T(8,128)(2,1)S(1)} all-gather(bf16[32,512]{1,0:T(8,128)(2,1)S(1)} %copy-done.5), channel_id=1, replica_groups=mesh['blk'=16,'mp'=2] {'blk'}, dimensions={0}, use_global_device_ids=true | all-gather | bytes 557056 | tf_op jit(solution)/shard_map/all_gather | solution.py:82
  54.0 1.0 copy.55
  55.0 37.9 %all_gather.10 = bf16[512,512]{1,0:T(8,128)(2,1)S(1)} all-gather(bf16[32,512]{1,0:T(8,128)(2,1)S(1)} %copy-done.6), channel_id=1, replica_groups=mesh['blk'=16,'mp'=2] {'blk'}, dimensions={0}, use_global_device_ids=true | all-gather | bytes 557056 | tf_op jit(solution)/shard_map/all_gather | solution.py:83
  93.1 0.8 copy.69
  94.0 1.8 pad_maximum_fusion
  96.1 1.9 fusion.26
  98.0 1.6 bitcast_reduce_fusion
  99.6 1.3 fusion.28
  100.9 1.7 fusion.21
  102.7 1.8 fusion.29
  104.5 4.5 %multiply_add_fusion.2 = f32[4,5,256,128]{3,2,1,0:T(8,128)} fusion(f32[4,5,256,128]{3,2,1,0:T(8,128)S(1)} %fusion.29, bf16[512,4,128,1]{0,2,3,1:T(8,128)(2,1)S(1)} %bitcast.95, f32[4,512,256,5]{2,1,3,0:T(8,128)S(1)} %get-tuple-element.280, f32[4,5,256]{2,1,0:T(8,128)S(1)} %get-tuple-element.278, f32[4,5,256]{2,1,0:T(8,128)S(1)} %get-tuple-element.269, ...), kind=kOutput, calls=%fused_computation.40 | convolution fusion | flops 680919040 | bytes 16314368 | tf_op jit(solution)/shard_map/hgqk,khd->hgqd/dot_general | solution.py:66
  109.0 112.8 %while.20 = (s32[]{:T(128)}, f32[4,5,256]{2,1,0:T(8,128)S(1)}, f32[4,5,256]{2,1,0:T(8,128)S(1)}, f32[4,5,256,128]{3,2,1,0:T(8,128)}, bf16[2,256,512]{1,2,0:T(8,1...) while((s32[]{:T(128)}, f32[4,5,256]{2,1,0:T(8,128)S(1)}, ...), condition=%wide.region_10.11_spmd.clone, body=%wide.region_6.0_spmd.clone.sunk | while | flops 689724160 | bytes 48571192 | solution.py:106
  109.0 3.1 collective-permute-start
  112.4 21.0 %collective-permute-done = bf16[2,256,512]{1,2,0:T(8,128)(2,1)S(1)} collective-permute-done((bf16[2,256,512]{1,2,0:T(8,128)(2,1)S(1)}, bf16[2,256,512]{1,2,0:T(8,128)(2,1)S(1)}, u32[]{:S(2)}, u32[]{:S(2)}) %collective-permute-start) | collective-permute-done | bytes 524320 | tf_op jit(solution)/shard_map/while/body/eval_jaxpr/ppermute | solution.py:17
  133.4 1.0 fusion.68
  134.5 1.3 fusion.69
  135.8 2.4 multiply_add_fusion.7
  138.3 1.4 copy-done.1
  139.7 1.9 collective-permute-start
  141.9 9.0 %collective-permute-done = bf16[2,256,512]{1,2,0:T(8,128)(2,1)S(1)} collective-permute-done((bf16[2,256,512]{1,2,0:T(8,128)(2,1)S(1)}, bf16[2,256,512]{1,2,0:T(8,128)(2,1)S(1)}, u32[]{:S(2)}, u32[]{:S(2)}) %collective-permute-start) | collective-permute-done | bytes 524320 | tf_op jit(solution)/shard_map/while/body/eval_jaxpr/ppermute | solution.py:17
  151.0 1.0 fusion.68
  152.1 1.3 fusion.69
  153.4 2.4 multiply_add_fusion.7
  155.8 1.4 copy-done.1
  157.3 13.1 %collective-permute-start = (bf16[2,256,512]{1,2,0:T(8,128)(2,1)S(1)}, bf16[2,256,512]{1,2,0:T(8,128)(2,1)S(1)}, u32[]{:S(2)}, u32[]{:S(2)}) collective-permute-start(bf16[2,256,512]{1,2,0:T(8,128)(2,1)S(1)} %get-tuple-element.376), channel_id=1, source_target_pairs={{0,2},{2,4},{4,6},{6,8},{8,10},{10,12},{12,14},{14,16},{16,18},{18... | collective-permute-start | bytes 1572872 | tf_op jit(solution)/shard_map/while/body/eval_jaxpr/ppermute | solution.py:17
  170.6 7.0 %collective-permute-done = bf16[2,256,512]{1,2,0:T(8,128)(2,1)S(1)} collective-permute-done((bf16[2,256,512]{1,2,0:T(8,128)(2,1)S(1)}, bf16[2,256,512]{1,2,0:T(8,128)(2,1)S(1)}, u32[]{:S(2)}, u32[]{:S(2)}) %collective-permute-start) | collective-permute-done | bytes 524320 | tf_op jit(solution)/shard_map/while/body/eval_jaxpr/ppermute | solution.py:17
  177.6 1.0 fusion.68
  178.7 1.3 fusion.69
  180.2 2.4 multiply_add_fusion.7
  182.6 1.4 copy-done.1
  184.0 13.0 %collective-permute-start = (bf16[2,256,512]{1,2,0:T(8,128)(2,1)S(1)}, bf16[2,256,512]{1,2,0:T(8,128)(2,1)S(1)}, u32[]{:S(2)}, u32[]{:S(2)}) collective-permute-start(bf16[2,256,512]{1,2,0:T(8,128)(2,1)S(1)} %get-tuple-element.376), channel_id=1, source_target_pairs={{0,2},{2,4},{4,6},{6,8},{8,10},{10,12},{12,14},{14,16},{16,18},{18... | collective-permute-start | bytes 1572872 | tf_op jit(solution)/shard_map/while/body/eval_jaxpr/ppermute | solution.py:17
  197.3 18.3 %collective-permute-done = bf16[2,256,512]{1,2,0:T(8,128)(2,1)S(1)} collective-permute-done((bf16[2,256,512]{1,2,0:T(8,128)(2,1)S(1)}, bf16[2,256,512]{1,2,0:T(8,128)(2,1)S(1)}, u32[]{:S(2)}, u32[]{:S(2)}) %collective-permute-start) | collective-permute-done | bytes 524320 | tf_op jit(solution)/shard_map/while/body/eval_jaxpr/ppermute | solution.py:17
  215.6 1.0 fusion.68
  216.7 1.3 fusion.69
  218.0 2.4 multiply_add_fusion.7
  220.5 1.4 copy-done.1
  221.9 2.1 copy.70
  224.0 1.3 divide_convert_fusion
  225.4 119.0 %all-gather.2.cloned.1.call-done = bf16[2560,5120]{0,1:T(8,128)(2,1)} async-done(((bf16[2560,320]{0,1:T(8,128)(2,1)}), bf16[2560,5120]{0,1:T(8,128)(2,1)}) %all-gather.2.cloned.1.call-update) | async-done | bytes 26214416 | tf_op jit(solution)/shard_map/all_gather | solution.py:116
  344.4 13.5 %convolution_convert_fusion = bf16[256,5120]{1,0:T(8,128)(2,1)} fusion(bf16[256,2560]{0,1:T(8,128)(2,1)} %bitcast.97, bf16[2560,5120]{0,1:T(8,128)(2,1)} %all-gather.2.cloned.1.call-done), kind=kOutput, calls=%fused_computation.29 | convolution fusion | flops 6712197120 | bytes 30146560 | tf_op jit(solution)/shard_map/dot_general | solution.py:114
  357.9 10.8 %reduce-scatter.2.cloned.1.call-done = bf16[256,2560]{1,0:T(8,128)(2,1)} async-done(((bf16[256,5120]{1,0:T(8,128)(2,1)}), bf16[256,2560]{1,0:T(8,128)(2,1)}) %reduce-scatter.2.cloned.1.call-update) | async-done | bytes 1310736 | tf_op jit(solution)/shard_map/reduce_scatter | solution.py:119
  (70 shorter events, 2.4 us)
Async XLA Ops:
  6.5 9.6 %copy-start.5 = (bf16[32,512]{1,0:T(8,128)(2,1)S(1)}, bf16[32,512]{1,0:T(8,128)(2,1)}, u32[]{:S(2)}) copy-start(bf16[32,512]{1,0:T(8,128)(2,1)} %param.12) | copy-start | bytes 98308
  6.5 48.5 %copy-start.6 = (bf16[32,512]{1,0:T(8,128)(2,1)S(1)}, bf16[32,512]{1,0:T(8,128)(2,1)}, u32[]{:S(2)}) copy-start(bf16[32,512]{1,0:T(8,128)(2,1)} %param.13) | copy-start | bytes 98308
  6.5 337.8 %all-gather.2.cloned.1.call-start = ((), (), s32[]{:S(2)}) async-start(), calls=%async_computation.1 | async-start | bytes 27852800 | tf_op jit(solution)/shard_map/all_gather | solution.py:116
  7.3 361.5 %reduce-scatter.2.cloned.1.call-start = ((), (), s32[]{:S(2)}) async-start(), calls=%async_computation.2 | async-start | bytes 3932160 | tf_op jit(solution)/shard_map/reduce_scatter | solution.py:119
  93.9 4.1 %copy-start.2 = (bf16[512,512]{0,1:T(8,128)(2,1)S(1)}, bf16[512,512]{0,1:T(8,128)(2,1)}, u32[]{:S(2)}) copy-start(bf16[512,512]{0,1:T(8,128)(2,1)} %copy.55) | copy-start | bytes 1572868
  100.9 1.8 copy-start.4
  104.5 4.5 %copy-start.3 = (bf16[2,256,512]{1,2,0:T(8,128)(2,1)S(1)}, bf16[2,256,512]{1,2,0:T(8,128)(2,1)}, u32[]{:S(2)}) copy-start(bf16[2,256,512]{1,2,0:T(8,128)(2,1)} %pad_maximum_fusion) | copy-start | bytes 1572868
  109.0 24.4 %collective-permute-start = (bf16[2,256,512]{1,2,0:T(8,128)(2,1)S(1)}, bf16[2,256,512]{1,2,0:T(8,128)(2,1)S(1)}, u32[]{:S(2)}, u32[]{:S(2)}) collective-permute-start(bf16[2,256,512]{1,2,0:T(8,128)(2,1)S(1)} %get-tuple-element.376), channel_id=1, source_target_pairs={{0,2},{2,4},{4,6},{6,8},{8,10},{10,12},{12,14},{14,16},{16,18},{18... | collective-permute-start | bytes 1572872 | tf_op jit(solution)/shard_map/while/body/eval_jaxpr/ppermute | solution.py:17
  133.4 2.4 copy-start
  138.2 1.5 copy-start.1
  139.7 11.2 %collective-permute-start = (bf16[2,256,512]{1,2,0:T(8,128)(2,1)S(1)}, bf16[2,256,512]{1,2,0:T(8,128)(2,1)S(1)}, u32[]{:S(2)}, u32[]{:S(2)}) collective-permute-start(bf16[2,256,512]{1,2,0:T(8,128)(2,1)S(1)} %get-tuple-element.376), channel_id=1, source_target_pairs={{0,2},{2,4},{4,6},{6,8},{8,10},{10,12},{12,14},{14,16},{16,18},{18... | collective-permute-start | bytes 1572872 | tf_op jit(solution)/shard_map/while/body/eval_jaxpr/ppermute | solution.py:17
  151.0 2.4 copy-start
  155.8 1.5 copy-start.1
  157.3 20.3 %collective-permute-start = (bf16[2,256,512]{1,2,0:T(8,128)(2,1)S(1)}, bf16[2,256,512]{1,2,0:T(8,128)(2,1)S(1)}, u32[]{:S(2)}, u32[]{:S(2)}) collective-permute-start(bf16[2,256,512]{1,2,0:T(8,128)(2,1)S(1)} %get-tuple-element.376), channel_id=1, source_target_pairs={{0,2},{2,4},{4,6},{6,8},{8,10},{10,12},{12,14},{14,16},{16,18},{18... | collective-permute-start | bytes 1572872 | tf_op jit(solution)/shard_map/while/body/eval_jaxpr/ppermute | solution.py:17
  177.6 2.5 copy-start
  182.5 1.5 copy-start.1
  184.0 31.6 %collective-permute-start = (bf16[2,256,512]{1,2,0:T(8,128)(2,1)S(1)}, bf16[2,256,512]{1,2,0:T(8,128)(2,1)S(1)}, u32[]{:S(2)}, u32[]{:S(2)}) collective-permute-start(bf16[2,256,512]{1,2,0:T(8,128)(2,1)S(1)} %get-tuple-element.376), channel_id=1, source_target_pairs={{0,2},{2,4},{4,6},{6,8},{8,10},{10,12},{12,14},{14,16},{16,18},{18... | collective-permute-start | bytes 1572872 | tf_op jit(solution)/shard_map/while/body/eval_jaxpr/ppermute | solution.py:17
  215.6 2.4 copy-start
  220.4 1.5 copy-start.1
Sparse Core Ops, SparseCore 0:
  10.1 334.2 all-gather.1
  358.1 10.6 reduce-scatter.1
where the time goes:
time: 377 us; the launch traced here: 376 us
  waiting for transfers between devices  186 us (49%)
  blocking collectives  75.8 us (20%)
  matrix products  37.1 us (10%)
  starting transfers between devices  31.1 us (8%)
  local copies, waits for them, and re-layouts  19 us (5%)
  between operations  13.6 us (4%)
  other arithmetic  12.9 us (3%)
    all_gather x1, waiting for transfers between devices, per_device(): lax.all_gather(out_weight, 'blk', axis=1, tiled=True)  119 us
    ppermute x4, waiting for transfers between devices, passed_along(): return lax.ppermute(block, axis, route)  55.2 us
    all_gather x1, blocking collectives, per_device(): lax.all_gather(shared_prefix_values, 'blk', axis=0, tiled=True)  37.9 us
    all_gather x1, blocking collectives, per_device(): lax.all_gather(shared_prefix_keys, 'blk', axis=0, tiled=True)  37.9 us
    ppermute x4, starting transfers between devices, passed_along(): return lax.ppermute(block, axis, route)  31 us
    dot_general x6, matrix products, update(): jnp.einsum('hgqk,khd->hgqd', weights.astype(jnp.bfloat16), value_heads, p...  15.9 us
    dot_general x1, matrix products, per_device(): jnp.dot(attn, lax.all_gather(out_weight, 'blk', axis=1, tiled=True), pref...  13.5 us
    reduce_scatter x1, waiting for transfers between devices, per_device(): lax.psum_scatter(product.astype(jnp.bfloat16), 'mp', scatter_dimension=1,...  10.8 us
  transfers between devices with their start and end apart: 6, of which 6 were waited for; matrix products, arithmetic and copies ran while one was open for 13% of the time, Pallas kernels for 0%

commit v1 on v0

--- a/solution.py
+++ b/solution.py
@@ -3,6 +3,8 @@
 import jax
 import jax.numpy as jnp
 from jax import lax
+from jax.experimental import pallas as pl
+from jax.experimental.pallas import tpu as pltpu
 from jax.sharding import PartitionSpec as P
 
 HEAD_SIZE = 128
@@ -119,7 +121,375 @@
     return lax.psum_scatter(product.astype(jnp.bfloat16), "mp", scatter_dimension=1, tiled=True)
 
 
+MESH = pl.DeviceIdType.MESH
+NT = (((1,), (1,)), ((), ()))
+REACH = 4
+PLANE = 4
+
+
+def fused_kernel(
+    q_ref, k_ref, v_ref, pk_ref, pv_ref, w_ref, len_ref,
+    out_ref,
+    keys, values, bias, weights, attn, mine, to_core, from_core, summed,
+    pz_s, pz_r, pp_s, pp_r, sx_s, sx_r, w_s, w_r, at_s, at_r, mp_s, mp_r, out_s, out_r,
+):
+    rows = q_ref.shape[0]
+    kv_heads = k_ref.shape[1] // HEAD_SIZE
+    group = q_ref.shape[1] // k_ref.shape[1]
+    part = pk_ref.shape[0]
+    prefix = part * PLANE * PLANE
+    chunk = part * PLANE
+    me = lax.axis_index("blk")
+    mp = lax.axis_index("mp")
+    z = lax.div(me, PLANE)
+    i = lax.rem(me, PLANE)
+
+    def send(src, dst, send_sem, recv_sem, blk, core=None):
+        return pltpu.make_async_remote_copy(
+            src_ref=src, dst_ref=dst, send_sem=send_sem, recv_sem=recv_sem,
+            device_id=(blk, mp if core is None else core), device_id_type=MESH,
+        )
+
+    def in_column(o):
+        return lax.rem(z + o, PLANE) * PLANE + i
+
+    def in_plane(o):
+        return z * PLANE + lax.rem(i + o, PLANE)
+
+    barrier = pltpu.get_barrier_semaphore()
+    for o in (1, 2, 3):
+        pl.semaphore_signal(barrier, inc=1, device_id=(in_column(o), mp), device_id_type=MESH)
+        pl.semaphore_signal(barrier, inc=1, device_id=(in_plane(o), mp), device_id_type=MESH)
+    pl.semaphore_signal(barrier, inc=1, device_id=(me, 1 - mp), device_id_type=MESH)
+    pl.semaphore_wait(barrier, 7)
+
+    kv = ((k_ref, pk_ref, keys), (v_ref, pv_ref, values))
+
+    def suffix_rows(d):
+        return pl.ds(prefix + d * rows, rows)
+
+    def up_copy(c):
+        own, _, held = kv[c]
+        return send(own, held.at[suffix_rows(REACH)], sx_s.at[REACH, c], sx_r.at[REACH, c],
+                    me + REACH)
+
+    own_rows = pl.ds(pl.multiple_of(i * chunk + z * part, part), part)
+
+    def prefix_up(o, c):
+        _, own, held = kv[c]
+        return send(own, held.at[own_rows], pz_s.at[o, c], pz_r.at[o, c], in_column(o))
+
+    my_chunk = pl.ds(pl.multiple_of(i * chunk, chunk), chunk)
+
+    def prefix_across(o, c):
+        held = kv[c][2]
+        return send(held.at[my_chunk], held.at[my_chunk], pp_s.at[o, c], pp_r.at[o, c],
+                    in_plane(o))
+
+    def across_own(d, c):
+        own, _, held = kv[c]
+        return send(own, held.at[suffix_rows(d)], sx_s.at[d, c], sx_r.at[d, c], in_plane(d))
+
+    def across_relayed(d, c):
+        held = kv[c][2]
+        return send(held.at[suffix_rows(REACH)], held.at[suffix_rows(d)], sx_s.at[d, c],
+                    sx_r.at[d, c], in_plane(d))
+
+    def weight_hop(way, k):
+        origin = z - (k - 1) if way == 0 else z + (k - 1)
+        to = me + PLANE if way == 0 else me - PLANE
+        source = w_ref if k == 1 else weights.at[origin]
+        return send(source, weights.at[origin], w_s.at[way, k], w_r.at[way, k], to)
+
+    def sends_hop(way, k):
+        if way == 0:
+            return (z - (k - 1) >= 0) & (z + 1 < PLANE)
+        return (z + (k - 1) < PLANE) & (z >= 1)
+
+    def gets_hop(way, k):
+        return z - k >= 0 if way == 0 else z + k < PLANE
+
+    def start_hop(k):
+        for way in (0, 1):
+            @pl.when(sends_hop(way, k))
+            def _():
+                weight_hop(way, k).start()
+
+    def take_hop(k):
+        for way in (0, 1):
+            @pl.when(gets_hop(way, k))
+            def _():
+                weight_hop(way, k).wait_recv()
+
+    for o in (1, 2, 3):
+        for c in (0, 1):
+            prefix_up(o, c).start()
+
+    @pl.when(z + 1 < PLANE)
+    def _():
+        up_copy(0).start()
+        up_copy(1).start()
+
+    for d in (1, 2, 3):
+        @pl.when(i + d < PLANE)
+        def _():
+            across_own(d, 0).start()
+            across_own(d, 1).start()
+
+    start_hop(1)
+
+    keys[own_rows, :] = pk_ref[...]
+    values[own_rows, :] = pv_ref[...]
+    keys[pl.ds(prefix, rows), :] = k_ref[...]
+    values[pl.ds(prefix, rows), :] = v_ref[...]
+    weights[z] = w_ref[...]
+    for d in range(1, REACH + 1):
+        @pl.when(me < d)
+        def _():
+            keys[suffix_rows(d), :] = jnp.zeros((rows, keys.shape[1]), keys.dtype)
+            values[suffix_rows(d), :] = jnp.zeros((rows, keys.shape[1]), keys.dtype)
+
+    query_pos = me * rows + lax.broadcasted_iota(jnp.int32, (rows, HEAD_SIZE), 0)
+    first = jnp.zeros((rows, HEAD_SIZE), jnp.int32)
+    end = jnp.int32(0)
+    for r in range(len_ref.shape[0]):
+        end = end + len_ref[r]
+        first = jnp.maximum(first, jnp.where(query_pos >= end, end, 0))
+    lane = lax.broadcasted_iota(jnp.int32, (rows, HEAD_SIZE), 1)
+    for d in range(REACH + 1):
+        for t in range(rows // HEAD_SIZE):
+            key_pos = (me - d) * rows + t * HEAD_SIZE + lane
+            seen = (key_pos >= first) & (key_pos <= query_pos)
+            at = d * rows + t * HEAD_SIZE
+            bias[:, at:at + HEAD_SIZE] = jnp.where(seen, 0.0, MASKED_SCORE)
+
+    for o in (1, 2, 3):
+        for c in (0, 1):
+            prefix_up(o, c).wait_recv()
+    for o in (1, 2, 3):
+        for c in (0, 1):
+            prefix_across(o, c).start()
+
+    @pl.when(z >= 1)
+    def _():
+        up_copy(0).wait_recv()
+        up_copy(1).wait_recv()
+        for d in (1, 2, 3):
+            @pl.when(i + d >= PLANE)
+            def _():
+                across_relayed(d, 0).start()
+                across_relayed(d, 1).start()
+
+    for o in (1, 2, 3):
+        for c in (0, 1):
+            prefix_across(o, c).wait_recv()
+    for d in (1, 2, 3):
+        @pl.when(me >= d)
+        def _():
+            across_own(d, 0).wait_recv()
+            across_own(d, 1).wait_recv()
+
+    exponent_scale = math.log2(math.e) / math.sqrt(HEAD_SIZE)
+    width = group * HEAD_SIZE
+
+    def attn_part(g, o):
+        columns = pl.ds(pl.multiple_of(g * width, HEAD_SIZE), width)
+        block = attn.at[i, :, columns]
+        return send(block, block, at_s.at[g, o], at_r.at[g, o], in_plane(o))
+
+    def one_group(g, carry):
+        head = pl.ds(pl.multiple_of(g * HEAD_SIZE, HEAD_SIZE), HEAD_SIZE)
+        for h in range(group):
+            column = pl.ds(pl.multiple_of(g * width + h * HEAD_SIZE, HEAD_SIZE), HEAD_SIZE)
+            q = q_ref[:, column]
+            s_pre = lax.dot_general(q, keys[:prefix, head], NT, preferred_element_type=jnp.float32)
+            s_suf = lax.dot_general(q, keys[prefix:, head], NT, preferred_element_type=jnp.float32)
+            s_suf = s_suf + bias[...]
+            peak = jnp.maximum(
+                jnp.max(s_pre, axis=1, keepdims=True), jnp.max(s_suf, axis=1, keepdims=True)
+            )
+            p_pre = jnp.exp2((s_pre - peak) * exponent_scale)
+            p_suf = jnp.exp2((s_suf - peak) * exponent_scale)
+            total = jnp.sum(p_pre, axis=1, keepdims=True) + jnp.sum(p_suf, axis=1, keepdims=True)
+            mixed = jnp.dot(
+                p_pre.astype(jnp.bfloat16), values[:prefix, head],
+                preferred_element_type=jnp.float32,
+            ) + jnp.dot(
+                p_suf.astype(jnp.bfloat16), values[prefix:, head],
+                preferred_element_type=jnp.float32,
+            )
+            attn[i, :, column] = (mixed / total).astype(jnp.bfloat16)
+        for o in (1, 2, 3):
+            attn_part(g, o).start()
+
+        @pl.when(g == 1)
+        def _():
+            take_hop(1)
+            start_hop(2)
+
+        return carry
+
+    lax.fori_loop(0, kv_heads, one_group, 0)
+
+    take_hop(2)
+    start_hop(3)
+
+    def take_attn(g, carry):
+        for o in (1, 2, 3):
+            attn_part(g, o).wait_recv()
+        return carry
+
+    lax.fori_loop(0, kv_heads, take_attn, 0)
+
+    def to_sibling(low, t):
+        return send(to_core.at[low, t], from_core.at[low, t], mp_s.at[low, t], mp_r.at[low, t],
+                    me, 1 - mp)
+
+    def to_owner(low, t):
+        return send(summed.at[low, t], out_ref.at[low * PLANE + i], out_s.at[low, t],
+                    out_r.at[low, i], z * PLANE + t)
+
+    def out_arrival(low, t):
+        return send(summed.at[low, t], out_ref.at[low * PLANE + t], out_s.at[low, t],
+                    out_r.at[low, t], z * PLANE + t)
+
+    def one_shard(n, carry):
+        inner = lax.div(z * (3 - z), 2)
+        f = n + inner * (1 - 2 * n) * (1 - lax.div(n, 2))
+        src = f + lax.div(z, 2) * (3 - 2 * f)
+        low = lax.rem(src, 2)
+        ours = lax.div(src, 2) == mp
+
+        @pl.when(n == 3)
+        def _():
+            take_hop(3)
+
+        def one_block(t, c):
+            product = lax.dot_general(
+                attn[t], weights[src], NT, preferred_element_type=jnp.float32
+            ).astype(jnp.bfloat16)
+
+            @pl.when(ours)
+            def _():
+                mine[t] = product
+
+            @pl.when(jnp.logical_not(ours))
+            def _():
+                to_core[low, t] = product
+                to_sibling(low, t).start()
+
+            return c
+
+        lax.fori_loop(0, PLANE, one_block, 0)
+
+        @pl.when(ours)
+        def _():
+            def add_block(t, c):
+                to_sibling(low, t).wait_recv()
+                both = mine[t].astype(jnp.float32) + from_core[low, t].astype(jnp.float32)
+                both = both.astype(jnp.bfloat16)
+
+                @pl.when(t == i)
+                def _():
+                    out_ref[low * PLANE + i] = both
+
+                @pl.when(t != i)
+                def _():
+                    summed[low, t] = both
+                    to_owner(low, t).start()
+
+                return c
+
+            lax.fori_loop(0, PLANE, add_block, 0)
+
+        return carry
+
+    lax.fori_loop(0, PLANE, one_shard, 0)
+
+    for low in (0, 1):
+        for t in range(PLANE):
+            to_sibling(low, t).wait_send()
+
+            @pl.when(t != i)
+            def _():
+                out_arrival(low, t).wait_recv()
+                out_arrival(low, t).wait_send()
+
+    for o in (1, 2, 3):
+        for c in (0, 1):
+            prefix_up(o, c).wait_send()
+            prefix_across(o, c).wait_send()
+            across_own_sent = across_own(o, c)
+
+            @pl.when((i + o < PLANE) | (z >= 1))
+            def _():
+                across_own_sent.wait_send()
+        for g in range(kv_heads):
+            attn_part(g, o).wait_send()
+    for c in (0, 1):
+        @pl.when(z + 1 < PLANE)
+        def _():
+            up_copy(c).wait_send()
+    for k in (1, 2, 3):
+        for way in (0, 1):
+            @pl.when(sends_hop(way, k))
+            def _():
+                weight_hop(way, k).wait_send()
+
+
+def per_device_fused(
+    queries,
+    suffix_key_rows,
+    suffix_value_rows,
+    shared_prefix_keys,
+    shared_prefix_values,
+    out_weight,
+    lengths,
+):
+    rows, q_cols = queries.shape
+    kv_cols = suffix_key_rows.shape[1]
+    columns = out_weight.shape[1]
+    held = shared_prefix_keys.shape[0] * PLANE * PLANE + (REACH + 1) * rows
+    kv_heads = kv_cols // HEAD_SIZE
+    vmem = pl.BlockSpec(memory_space=pltpu.VMEM)
+    low = jnp.bfloat16
+    sem = pltpu.SemaphoreType.DMA
+    blocks = pl.pallas_call(
+        fused_kernel,
+        out_shape=jax.ShapeDtypeStruct((2 * PLANE, rows, columns), low),
+        in_specs=[vmem] * 6 + [pl.BlockSpec(memory_space=pltpu.SMEM)],
+        out_specs=vmem,
+        scratch_shapes=[
+            pltpu.VMEM((held, kv_cols), low),
+            pltpu.VMEM((held, kv_cols), low),
+            pltpu.VMEM((rows, (REACH + 1) * rows), jnp.float32),
+            pltpu.VMEM((PLANE, columns, q_cols), low),
+            pltpu.VMEM((PLANE, rows, q_cols), low),
+            pltpu.VMEM((PLANE, rows, columns), low),
+            pltpu.VMEM((2, PLANE, rows, columns), low),
+            pltpu.VMEM((2, PLANE, rows, columns), low),
+            pltpu.VMEM((2, PLANE, rows, columns), low),
+            sem((4, 2)), sem((4, 2)), sem((4, 2)), sem((4, 2)),
+            sem((REACH + 1, 2)), sem((REACH + 1, 2)),
+            sem((2, 4)), sem((2, 4)),
+            sem((kv_heads, 4)), sem((kv_heads, 4)),
+            sem((2, PLANE)), sem((2, PLANE)), sem((2, PLANE)), sem((2, PLANE)),
+        ],
+        compiler_params=pltpu.CompilerParams(
+            collective_id=0, has_side_effects=True, vmem_limit_bytes=52 * 1024 * 1024
+        ),
+        cost_estimate=pl.CostEstimate(
+            flops=12_000_000_000, bytes_accessed=8_000_000, transcendentals=10_000_000
+        ),
+    )(
+        queries, suffix_key_rows, suffix_value_rows, shared_prefix_keys, shared_prefix_values,
+        out_weight.T, lengths,
+    )
+    return jnp.transpose(blocks, (1, 0, 2)).reshape(rows, 2 * PLANE * columns)
+
+
 def solution(mesh):
+    fused = mesh.shape["mp"] == 2 and mesh.shape["blk"] == PLANE * PLANE
     placed = (
         P("blk", "mp"),
         P("blk", "mp"),
@@ -130,5 +500,5 @@
         P(),
     )
     return jax.shard_map(
-        per_device, mesh=mesh, in_specs=placed, out_specs=P("blk", "mp"), check_vma=False
-    )
+        per_device_fused if fused else per_device, mesh=mesh, in_specs=placed, out_specs=P("blk", "mp"), check_vma=False
+    )

time: 377 us -> 153 us (0.41)
  waiting for transfers between devices: 186 us -> 0 us
  Pallas kernels: 0 us -> 144 us
  blocking collectives: 75.8 us -> 0 us
  matrix products: 37.1 us -> 0 us
  starting transfers between devices: 31.1 us -> 0 us
  between operations: 13.6 us -> 0.02 us
  other arithmetic: 12.9 us -> 0 us
  local copies, waits for them, and re-layouts: 19 us -> 8.67 us
    pallas_call x0 -> x1, Pallas kernels: none -> 144 us  [per_device_fused(): pl.pallas_call(fused_kernel, out_shape=jax.ShapeDtypeStruct((2 * PLANE, r...]
    all_gather x1 -> x0, waiting for transfers between devices: 119 us -> none  [per_device(): lax.all_gather(out_weight, 'blk', axis=1, tiled=True)]
    all_gather x2 -> x0, blocking collectives: 75.8 us -> none  [the longest x1 37.9 us: per_device(): lax.all_gather(shared_prefix_values, 'blk', axis=0, tiled=True)]
    ppermute x4 -> x0, waiting for transfers between devices: 55.2 us -> none  [passed_along(): return lax.ppermute(block, axis, route)]
    dot_general x13 -> x0, matrix products: 37.1 us -> none  [the longest x6 15.9 us: update(): jnp.einsum('hgqk,khd->hgqd', weights.astype(jnp.bfloat16), value_heads, p...]
    ppermute x4 -> x0, starting transfers between devices: 31 us -> none  [passed_along(): return lax.ppermute(block, axis, route)]
    reduce_scatter x1 -> x0, waiting for transfers between devices: 10.8 us -> none  [per_device(): lax.psum_scatter(product.astype(jnp.bfloat16), 'mp', scatter_dimension=1,...]
    reduce_sum x11 -> x0, other arithmetic: 8.54 us -> none  [the longest x6 8.1 us: update(): row_total = row_total * rescale + jnp.sum(weights, axis=-1)]
  transfers between devices with their start and end apart: 6 -> 0, of which waited for: 6 -> 0; matrix products, arithmetic and copies ran while one was open for 13% -> 0% of each run, Pallas kernels for 0% -> 0%
where the time goes in v1:
time: 153 us; the launch traced here: 152 us
  Pallas kernels  144 us (94%)
  local copies, waits for them, and re-layouts  8.67 us (6%)
    pallas_call x1, Pallas kernels, per_device_fused(): pl.pallas_call(fused_kernel, out_shape=jax.ShapeDtypeStruct((2 * PLANE, r...  144 us
    unnamed x12, local copies, waits for them, and re-layouts  5.38 us

profile of v1, /device:TPU:5, one launch (start us, length us, event | category | flops | bytes accessed | tf_op | source)
XLA Modules:
  0.0 152.4 jit_solution(2685713891229151358)
XLA Ops:
  0.0 0.0 copy-start
  0.0 1.3 copy-done
  1.3 0.0 copy-start.1
  1.3 0.9 copy-done.1
  2.3 0.0 copy-start.2
  2.3 0.9 copy-done.2
  3.2 0.0 copy-start.3
  3.2 0.8 copy-done.3
  4.0 0.0 copy-start.4
  4.0 0.8 copy-done.4
  4.7 0.0 copy-start.5
  4.7 0.7 copy-done.5
  5.4 143.7 %shard_map.73 = bf16[8,256,320]{2,1,0:T(8,128)(2,1)} custom-call(bf16[256,2560]{1,0:T(8,128)(2,1)S(1)} %copy-done, bf16[256,512]{1,0:T(8,128)(2,1)S(1)} %copy-done.1, bf16[256,512]{1,0:T(8,128)(2,1)S(1)} %copy-done.2, bf16[32,512]{1,0:T(8,128)(2,1)S(1)} %copy-done.3, bf16[32,512]{1,0:T(8,128)(2,1)S(1)} %copy-done.4, bf16[320,2560]{1,0:T(8,128)(2,1)} %bitcast.5, ...), custom_call_target="tpu_custom_call" | custom-call | flops 12000000000 | bytes 8000000 | tf_op jit(solution)/shard_map/pallas_call | solution.py:457
  149.1 1.7 %copy.8 = bf16[256,8,320]{0,2,1:T(8,128)(2,1)S(1)} copy(bf16[256,8,320]{2,0,1:T(8,128)(2,1)} %bitcast.4) | data formatting | bytes 2621440 | tf_op jit(solution)/shard_map/transpose | solution.py:488
  150.8 1.6 %copy.9 = bf16[256,2560]{1,0:T(8,128)(2,1)} copy(bf16[256,2560]{0,1:T(8,128)(2,1)S(1)} %bitcast.3) | data formatting | bytes 2621440 | tf_op jit(solution)/shard_map/reshape | solution.py:488
Async XLA Ops:
  0.0 1.3 copy-start
  1.3 0.9 copy-start.1
  2.3 0.9 copy-start.2
  3.2 0.8 copy-start.3
  4.0 0.8 copy-start.4
  4.7 0.7 copy-start.5

commit v2 on v1

--- a/solution.py
+++ b/solution.py
@@ -125,13 +125,14 @@
 NT = (((1,), (1,)), ((), ()))
 REACH = 4
 PLANE = 4
+PIECES = 4
 
 
 def fused_kernel(
     q_ref, k_ref, v_ref, pk_ref, pv_ref, w_ref, len_ref,
     out_ref,
-    keys, values, bias, weights, attn, mine, to_core, from_core, summed,
-    pz_s, pz_r, pp_s, pp_r, sx_s, sx_r, w_s, w_r, at_s, at_r, mp_s, mp_r, out_s, out_r,
+    queries, keys, values, bias, weights, attn, mine, to_core, from_core, summed,
+    local, pz_s, pz_r, pp_s, pp_r, sx_s, sx_r, w_s, w_r, at_s, at_r, mp_s, mp_r, out_s, out_r,
 ):
     rows = q_ref.shape[0]
     kv_heads = k_ref.shape[1] // HEAD_SIZE
@@ -143,6 +144,18 @@
     mp = lax.axis_index("mp")
     z = lax.div(me, PLANE)
     i = lax.rem(me, PLANE)
+    z_hi, z_lo = lax.div(z, 2), lax.rem(z, 2)
+    y, x = lax.div(i, 2), lax.rem(i, 2)
+    x_mate = me + 1 - 2 * x
+    y_mate = me + 2 * (1 - 2 * y)
+    near = me + PLANE * (1 - 2 * z_lo)
+    far = me + 2 * PLANE * (1 - 2 * z_hi)
+    across = near + 1 - 2 * x
+    shard = z_hi * 2 + y
+    far_shard = (1 - z_hi) * 2 + y
+    token = z_lo * 2 + x
+    near_token = (1 - z_lo) * 2 + x
+    x_token = z_lo * 2 + 1 - x
 
     def send(src, dst, send_sem, recv_sem, blk, core=None):
         return pltpu.make_async_remote_copy(
@@ -160,8 +173,24 @@
     for o in (1, 2, 3):
         pl.semaphore_signal(barrier, inc=1, device_id=(in_column(o), mp), device_id_type=MESH)
         pl.semaphore_signal(barrier, inc=1, device_id=(in_plane(o), mp), device_id_type=MESH)
+    pl.semaphore_signal(barrier, inc=1, device_id=(across, mp), device_id_type=MESH)
     pl.semaphore_signal(barrier, inc=1, device_id=(me, 1 - mp), device_id_type=MESH)
-    pl.semaphore_wait(barrier, 7)
+
+    own_rows = pl.ds(pl.multiple_of(i * chunk + z * part, part), part)
+    own_copies = [
+        pltpu.make_async_copy(source, target, local.at[n])
+        for n, (source, target) in enumerate((
+            (pk_ref, keys.at[own_rows]),
+            (pv_ref, values.at[own_rows]),
+            (k_ref, keys.at[pl.ds(prefix, rows)]),
+            (v_ref, values.at[pl.ds(prefix, rows)]),
+            (q_ref, queries),
+            (w_ref, weights.at[shard]),
+        ))
+    ]
+    for copy in own_copies:
+        copy.start()
+    pl.semaphore_wait(barrier, 8)
 
     kv = ((k_ref, pk_ref, keys), (v_ref, pv_ref, values))
 
@@ -173,8 +202,6 @@
         return send(own, held.at[suffix_rows(REACH)], sx_s.at[REACH, c], sx_r.at[REACH, c],
                     me + REACH)
 
-    own_rows = pl.ds(pl.multiple_of(i * chunk + z * part, part), part)
-
     def prefix_up(o, c):
         _, own, held = kv[c]
         return send(own, held.at[own_rows], pz_s.at[o, c], pz_r.at[o, c], in_column(o))
@@ -195,31 +222,23 @@
         return send(held.at[suffix_rows(REACH)], held.at[suffix_rows(d)], sx_s.at[d, c],
                     sx_r.at[d, c], in_plane(d))
 
-    def weight_hop(way, k):
-        origin = z - (k - 1) if way == 0 else z + (k - 1)
-        to = me + PLANE if way == 0 else me - PLANE
-        source = w_ref if k == 1 else weights.at[origin]
-        return send(source, weights.at[origin], w_s.at[way, k], w_r.at[way, k], to)
-
-    def sends_hop(way, k):
-        if way == 0:
-            return (z - (k - 1) >= 0) & (z + 1 < PLANE)
-        return (z + (k - 1) < PLANE) & (z >= 1)
-
-    def gets_hop(way, k):
-        return z - k >= 0 if way == 0 else z + k < PLANE
-
-    def start_hop(k):
-        for way in (0, 1):
-            @pl.when(sends_hop(way, k))
-            def _():
-                weight_hop(way, k).start()
-
-    def take_hop(k):
-        for way in (0, 1):
-            @pl.when(gets_hop(way, k))
-            def _():
-                weight_hop(way, k).wait_recv()
+    piece = w_ref.shape[0] // PIECES
+
+    def to_far(c):
+        at = pl.ds(c * piece, piece)
+        return send(w_ref.at[at], weights.at[shard, at], w_s.at[0, c], w_r.at[0, c], far)
+
+    def to_y(c):
+        at = pl.ds(c * piece, piece)
+        return send(w_ref.at[at], weights.at[shard, at], w_s.at[1, c], w_r.at[1, c], y_mate)
+
+    def far_to_y(c):
+        block = weights.at[far_shard, pl.ds(c * piece, piece)]
+        return send(block, block, w_s.at[2, c], w_r.at[2, c], y_mate)
+
+    def pass_on(c):
+        to_far(c).wait_recv()
+        far_to_y(c).start()
 
     for o in (1, 2, 3):
         for c in (0, 1):
@@ -236,13 +255,6 @@
             across_own(d, 0).start()
             across_own(d, 1).start()
 
-    start_hop(1)
-
-    keys[own_rows, :] = pk_ref[...]
-    values[own_rows, :] = pv_ref[...]
-    keys[pl.ds(prefix, rows), :] = k_ref[...]
-    values[pl.ds(prefix, rows), :] = v_ref[...]
-    weights[z] = w_ref[...]
     for d in range(1, REACH + 1):
         @pl.when(me < d)
         def _():
@@ -263,6 +275,8 @@
             at = d * rows + t * HEAD_SIZE
             bias[:, at:at + HEAD_SIZE] = jnp.where(seen, 0.0, MASKED_SCORE)
 
+    for copy in own_copies:
+        copy.wait()
     for o in (1, 2, 3):
         for c in (0, 1):
             prefix_up(o, c).wait_recv()
@@ -280,6 +294,10 @@
                 across_relayed(d, 0).start()
                 across_relayed(d, 1).start()
 
+    for c in range(PIECES):
+        to_far(c).start()
+    to_y(0).start()
+
     for o in (1, 2, 3):
         for c in (0, 1):
             prefix_across(o, c).wait_recv()
@@ -288,20 +306,49 @@
         def _():
             across_own(d, 0).wait_recv()
             across_own(d, 1).wait_recv()
+    for c in range(1, PIECES):
+        to_y(c).start()
 
     exponent_scale = math.log2(math.e) / math.sqrt(HEAD_SIZE)
     width = group * HEAD_SIZE
 
-    def attn_part(g, o):
+    def attn_block(t, g):
         columns = pl.ds(pl.multiple_of(g * width, HEAD_SIZE), width)
-        block = attn.at[i, :, columns]
-        return send(block, block, at_s.at[g, o], at_r.at[g, o], in_plane(o))
+        return attn.at[t, :, columns]
+
+    def attn_to_x(g):
+        block = attn_block(token, g)
+        return send(block, block, at_s.at[g, 0], at_r.at[g, 0], x_mate)
+
+    def attn_to_near(g):
+        block = attn_block(token, g)
+        return send(block, block, at_s.at[g, 1], at_r.at[g, 1], near)
+
+    def near_to_x(g):
+        block = attn_block(near_token, g)
+        return send(block, block, at_s.at[g, 2], at_r.at[g, 2], x_mate)
+
+    def x_to_near(g):
+        block = attn_block(x_token, g)
+        return send(block, block, at_s.at[g, 2], at_r.at[g, 2], near)
+
+    def attn_pass_on(g):
+        attn_to_x(g).wait_recv()
+        attn_to_near(g).wait_recv()
+
+        @pl.when(lax.rem(g, 2) == 0)
+        def _():
+            near_to_x(g).start()
+
+        @pl.when(lax.rem(g, 2) == 1)
+        def _():
+            x_to_near(g).start()
 
     def one_group(g, carry):
         head = pl.ds(pl.multiple_of(g * HEAD_SIZE, HEAD_SIZE), HEAD_SIZE)
         for h in range(group):
             column = pl.ds(pl.multiple_of(g * width + h * HEAD_SIZE, HEAD_SIZE), HEAD_SIZE)
-            q = q_ref[:, column]
+            q = queries[:, column]
             s_pre = lax.dot_general(q, keys[:prefix, head], NT, preferred_element_type=jnp.float32)
             s_suf = lax.dot_general(q, keys[prefix:, head], NT, preferred_element_type=jnp.float32)
             s_suf = s_suf + bias[...]
@@ -318,51 +365,60 @@
                 p_suf.astype(jnp.bfloat16), values[prefix:, head],
                 preferred_element_type=jnp.float32,
             )
-            attn[i, :, column] = (mixed / total).astype(jnp.bfloat16)
-        for o in (1, 2, 3):
-            attn_part(g, o).start()
-
-        @pl.when(g == 1)
-        def _():
-            take_hop(1)
-            start_hop(2)
+            attn[token, :, column] = (mixed / total).astype(jnp.bfloat16)
+        attn_to_x(g).start()
+        attn_to_near(g).start()
+
+        @pl.when(g >= 1)
+        def _():
+            attn_pass_on(g - 1)
 
         return carry
 
     lax.fori_loop(0, kv_heads, one_group, 0)
-
-    take_hop(2)
-    start_hop(3)
-
-    def take_attn(g, carry):
-        for o in (1, 2, 3):
-            attn_part(g, o).wait_recv()
+    attn_pass_on(jnp.int32(kv_heads - 1))
+    for c in range(PIECES):
+        pass_on(c)
+
+    def take_across(g, carry):
+        near_to_x(g).wait_recv()
         return carry
 
-    lax.fori_loop(0, kv_heads, take_attn, 0)
+    lax.fori_loop(0, kv_heads, take_across, 0)
 
     def to_sibling(low, t):
         return send(to_core.at[low, t], from_core.at[low, t], mp_s.at[low, t], mp_r.at[low, t],
                     me, 1 - mp)
 
+    def member(t):
+        return (z_hi * 2 + lax.div(t, 2)) * PLANE + y * 2 + lax.rem(t, 2)
+
+    def column_block(t, low):
+        return lax.div(t, 2) * PLANE + low * 2 + lax.rem(t, 2)
+
     def to_owner(low, t):
-        return send(summed.at[low, t], out_ref.at[low * PLANE + i], out_s.at[low, t],
-                    out_r.at[low, i], z * PLANE + t)
+        return send(summed.at[low, t], out_ref.at[column_block(token, low)], out_s.at[low, t],
+                    out_r.at[low, token], member(t))
 
     def out_arrival(low, t):
-        return send(summed.at[low, t], out_ref.at[low * PLANE + t], out_s.at[low, t],
-                    out_r.at[low, t], z * PLANE + t)
+        return send(summed.at[low, t], out_ref.at[column_block(t, low)], out_s.at[low, t],
+                    out_r.at[low, t], member(t))
 
     def one_shard(n, carry):
-        inner = lax.div(z * (3 - z), 2)
-        f = n + inner * (1 - 2 * n) * (1 - lax.div(n, 2))
-        src = f + lax.div(z, 2) * (3 - 2 * f)
-        low = lax.rem(src, 2)
-        ours = lax.div(src, 2) == mp
+        hi = z_hi + lax.div(n, 2) * (1 - 2 * z_hi)
+        low = y + lax.rem(n, 2) * (1 - 2 * y)
+        src = hi * 2 + low
+        ours = hi == mp
+
+        @pl.when(n == 1)
+        def _():
+            for c in range(PIECES):
+                to_y(c).wait_recv()
 
         @pl.when(n == 3)
         def _():
-            take_hop(3)
+            for c in range(PIECES):
+                far_to_y(c).wait_recv()
 
         def one_block(t, c):
             product = lax.dot_general(
@@ -389,11 +445,11 @@
                 both = mine[t].astype(jnp.float32) + from_core[low, t].astype(jnp.float32)
                 both = both.astype(jnp.bfloat16)
 
-                @pl.when(t == i)
+                @pl.when(t == token)
                 def _():
-                    out_ref[low * PLANE + i] = both
-
-                @pl.when(t != i)
+                    out_ref[column_block(token, low)] = both
+
+                @pl.when(t != token)
                 def _():
                     summed[low, t] = both
                     to_owner(low, t).start()
@@ -410,7 +466,7 @@
         for t in range(PLANE):
             to_sibling(low, t).wait_send()
 
-            @pl.when(t != i)
+            @pl.when(t != token)
             def _():
                 out_arrival(low, t).wait_recv()
                 out_arrival(low, t).wait_send()
@@ -424,17 +480,18 @@
             @pl.when((i + o < PLANE) | (z >= 1))
             def _():
                 across_own_sent.wait_send()
-        for g in range(kv_heads):
-            attn_part(g, o).wait_send()
     for c in (0, 1):
         @pl.when(z + 1 < PLANE)
         def _():
             up_copy(c).wait_send()
-    for k in (1, 2, 3):
-        for way in (0, 1):
-            @pl.when(sends_hop(way, k))
-            def _():
-                weight_hop(way, k).wait_send()
+    for c in range(PIECES):
+        to_far(c).wait_send()
+        to_y(c).wait_send()
+        far_to_y(c).wait_send()
+    for g in range(kv_heads):
+        attn_to_x(g).wait_send()
+        attn_to_near(g).wait_send()
+        near_to_x(g).wait_send()
 
 
 def per_device_fused(
@@ -457,9 +514,10 @@
     blocks = pl.pallas_call(
         fused_kernel,
         out_shape=jax.ShapeDtypeStruct((2 * PLANE, rows, columns), low),
-        in_specs=[vmem] * 6 + [pl.BlockSpec(memory_space=pltpu.SMEM)],
+        in_specs=[pl.BlockSpec(memory_space=pl.ANY)] * 6 + [pl.BlockSpec(memory_space=pltpu.SMEM)],
         out_specs=vmem,
         scratch_shapes=[
+            pltpu.VMEM((rows, q_cols), low),
             pltpu.VMEM((held, kv_cols), low),
             pltpu.VMEM((held, kv_cols), low),
             pltpu.VMEM((rows, (REACH + 1) * rows), jnp.float32),
@@ -469,14 +527,14 @@
             pltpu.VMEM((2, PLANE, rows, columns), low),
             pltpu.VMEM((2, PLANE, rows, columns), low),
             pltpu.VMEM((2, PLANE, rows, columns), low),
-            sem((4, 2)), sem((4, 2)), sem((4, 2)), sem((4, 2)),
+            sem((6,)), sem((4, 2)), sem((4, 2)), sem((4, 2)), sem((4, 2)),
             sem((REACH + 1, 2)), sem((REACH + 1, 2)),
-            sem((2, 4)), sem((2, 4)),
-            sem((kv_heads, 4)), sem((kv_heads, 4)),
+            sem((3, PIECES)), sem((3, PIECES)),
+            sem((kv_heads, 3)), sem((kv_heads, 3)),
             sem((2, PLANE)), sem((2, PLANE)), sem((2, PLANE)), sem((2, PLANE)),
         ],
         compiler_params=pltpu.CompilerParams(
-            collective_id=0, has_side_effects=True, vmem_limit_bytes=52 * 1024 * 1024
+            collective_id=0, has_side_effects=True, vmem_limit_bytes=60 * 1024 * 1024
         ),
         cost_estimate=pl.CostEstimate(
             flops=12_000_000_000, bytes_accessed=8_000_000, transcendentals=10_000_000

time: 153 us -> 176 us (1.15)
  Pallas kernels: 144 us -> 171 us
  local copies, waits for them, and re-layouts: 8.67 us -> 3.29 us
    pallas_call x1, Pallas kernels: 144 us -> 171 us  [per_device_fused(): pl.pallas_call(fused_kernel, out_shape=jax.ShapeDtypeStruct((2 * PLANE, r...]
    unnamed x12 -> x0, local copies, waits for them, and re-layouts: 5.38 us -> none
where the time goes in v2:
time: 176 us; the launch traced here: 174 us
  Pallas kernels  171 us (97%)
  local copies, waits for them, and re-layouts  3.29 us (2%)
    pallas_call x1, Pallas kernels, per_device_fused(): pl.pallas_call(fused_kernel, out_shape=jax.ShapeDtypeStruct((2 * PLANE, r...  171 us

profile of v2, /device:TPU:5, one launch (start us, length us, event | category | flops | bytes accessed | tf_op | source)
XLA Modules:
  0.0 174.1 jit_solution(2371551945941858831)
XLA Ops:
  0.0 170.8 %shard_map.73 = bf16[8,256,320]{2,1,0:T(8,128)(2,1)} custom-call(bf16[256,2560]{1,0:T(8,128)(2,1)} %q_ref.1, bf16[256,512]{1,0:T(8,128)(2,1)} %k_ref.1, bf16[256,512]{1,0:T(8,128)(2,1)} %v_ref.1, bf16[32,512]{1,0:T(8,128)(2,1)} %pk_ref.1, bf16[32,512]{1,0:T(8,128)(2,1)} %pv_ref.1, bf16[320,2560]{1,0:T(8,128)(2,1)} %bitcast.5, s32[16]{0:T(128)} %len_ref.1), custom_call_target="tpu_custom_call" | custom-call | flops 12000000000 | bytes 8000000 | tf_op jit(solution)/shard_map/pallas_call | solution.py:514
  170.8 1.7 copy.8
  172.5 1.6 copy.9

commit v3 on v1

--- a/solution.py
+++ b/solution.py
@@ -130,8 +130,8 @@
 def fused_kernel(
     q_ref, k_ref, v_ref, pk_ref, pv_ref, w_ref, len_ref,
     out_ref,
-    keys, values, bias, weights, attn, mine, to_core, from_core, summed,
-    pz_s, pz_r, pp_s, pp_r, sx_s, sx_r, w_s, w_r, at_s, at_r, mp_s, mp_r, out_s, out_r,
+    queries, keys, values, bias, weights, attn, mine, to_core, from_core, summed,
+    local, pz_s, pz_r, pp_s, pp_r, sx_s, sx_r, w_s, w_r, at_s, at_r, mp_s, mp_r, out_s, out_r,
 ):
     rows = q_ref.shape[0]
     kv_heads = k_ref.shape[1] // HEAD_SIZE
@@ -161,6 +161,21 @@
         pl.semaphore_signal(barrier, inc=1, device_id=(in_column(o), mp), device_id_type=MESH)
         pl.semaphore_signal(barrier, inc=1, device_id=(in_plane(o), mp), device_id_type=MESH)
     pl.semaphore_signal(barrier, inc=1, device_id=(me, 1 - mp), device_id_type=MESH)
+
+    own_rows = pl.ds(pl.multiple_of(i * chunk + z * part, part), part)
+    own_copies = [
+        pltpu.make_async_copy(source, target, local.at[n])
+        for n, (source, target) in enumerate((
+            (pk_ref, keys.at[own_rows]),
+            (pv_ref, values.at[own_rows]),
+            (k_ref, keys.at[pl.ds(prefix, rows)]),
+            (v_ref, values.at[pl.ds(prefix, rows)]),
+            (q_ref, queries),
+            (w_ref, weights.at[z]),
+        ))
+    ]
+    for copy in own_copies:
+        copy.start()
     pl.semaphore_wait(barrier, 7)
 
     kv = ((k_ref, pk_ref, keys), (v_ref, pv_ref, values))
@@ -172,8 +187,6 @@
         own, _, held = kv[c]
         return send(own, held.at[suffix_rows(REACH)], sx_s.at[REACH, c], sx_r.at[REACH, c],
                     me + REACH)
-
-    own_rows = pl.ds(pl.multiple_of(i * chunk + z * part, part), part)
 
     def prefix_up(o, c):
         _, own, held = kv[c]
@@ -236,13 +249,6 @@
             across_own(d, 0).start()
             across_own(d, 1).start()
 
-    start_hop(1)
-
-    keys[own_rows, :] = pk_ref[...]
-    values[own_rows, :] = pv_ref[...]
-    keys[pl.ds(prefix, rows), :] = k_ref[...]
-    values[pl.ds(prefix, rows), :] = v_ref[...]
-    weights[z] = w_ref[...]
     for d in range(1, REACH + 1):
         @pl.when(me < d)
         def _():
@@ -263,6 +269,8 @@
             at = d * rows + t * HEAD_SIZE
             bias[:, at:at + HEAD_SIZE] = jnp.where(seen, 0.0, MASKED_SCORE)
 
+    for copy in own_copies:
+        copy.wait()
     for o in (1, 2, 3):
         for c in (0, 1):
             prefix_up(o, c).wait_recv()
@@ -280,6 +288,13 @@
                 across_relayed(d, 0).start()
                 across_relayed(d, 1).start()
 
+    @pl.when(z + 1 < PLANE)
+    def _():
+        up_copy(0).wait_send()
+        up_copy(1).wait_send()
+
+    start_hop(1)
+
     for o in (1, 2, 3):
         for c in (0, 1):
             prefix_across(o, c).wait_recv()
@@ -301,7 +316,7 @@
         head = pl.ds(pl.multiple_of(g * HEAD_SIZE, HEAD_SIZE), HEAD_SIZE)
         for h in range(group):
             column = pl.ds(pl.multiple_of(g * width + h * HEAD_SIZE, HEAD_SIZE), HEAD_SIZE)
-            q = q_ref[:, column]
+            q = queries[:, column]
             s_pre = lax.dot_general(q, keys[:prefix, head], NT, preferred_element_type=jnp.float32)
             s_suf = lax.dot_general(q, keys[prefix:, head], NT, preferred_element_type=jnp.float32)
             s_suf = s_suf + bias[...]
@@ -334,13 +349,6 @@
     take_hop(2)
     start_hop(3)
 
-    def take_attn(g, carry):
-        for o in (1, 2, 3):
-            attn_part(g, o).wait_recv()
-        return carry
-
-    lax.fori_loop(0, kv_heads, take_attn, 0)
-
     def to_sibling(low, t):
         return send(to_core.at[low, t], from_core.at[low, t], mp_s.at[low, t], mp_r.at[low, t],
                     me, 1 - mp)
@@ -353,58 +361,88 @@
         return send(summed.at[low, t], out_ref.at[low * PLANE + t], out_s.at[low, t],
                     out_r.at[low, t], z * PLANE + t)
 
-    def one_shard(n, carry):
+    def shard(n):
         inner = lax.div(z * (3 - z), 2)
         f = n + inner * (1 - 2 * n) * (1 - lax.div(n, 2))
         src = f + lax.div(z, 2) * (3 - 2 * f)
-        low = lax.rem(src, 2)
-        ours = lax.div(src, 2) == mp
-
-        @pl.when(n == 3)
-        def _():
-            take_hop(3)
-
-        def one_block(t, c):
-            product = lax.dot_general(
-                attn[t], weights[src], NT, preferred_element_type=jnp.float32
-            ).astype(jnp.bfloat16)
-
-            @pl.when(ours)
-            def _():
-                mine[t] = product
-
-            @pl.when(jnp.logical_not(ours))
-            def _():
-                to_core[low, t] = product
-                to_sibling(low, t).start()
-
+        return src, lax.rem(src, 2), lax.div(src, 2) == mp
+
+    def rows_from(o):
+        return lax.rem(i - o + PLANE, PLANE)
+
+    def multiply(n, t):
+        src, low, ours = shard(n)
+        product = lax.dot_general(
+            attn[t], weights[src], NT, preferred_element_type=jnp.float32
+        ).astype(jnp.bfloat16)
+
+        @pl.when(ours)
+        def _():
+            mine[low, t] = product
+
+        @pl.when(jnp.logical_not(ours))
+        def _():
+            to_core[low, t] = product
+            to_sibling(low, t).start()
+
+    def add(n, t):
+        src, low, ours = shard(n)
+
+        @pl.when(ours)
+        def _():
+            to_sibling(low, t).wait_recv()
+            both = mine[low, t].astype(jnp.float32) + from_core[low, t].astype(jnp.float32)
+            both = both.astype(jnp.bfloat16)
+
+            @pl.when(t == i)
+            def _():
+                out_ref[low * PLANE + i] = both
+
+            @pl.when(t != i)
+            def _():
+                summed[low, t] = both
+                to_owner(low, t).start()
+
+    def one_source(o, carry):
+        for v in (1, 2, 3):
+            @pl.when(o == v)
+            def _():
+                for g in range(kv_heads):
+                    attn_part(g, v).wait_recv()
+
+        def times(n, c):
+            multiply(n, rows_from(o))
             return c
 
-        lax.fori_loop(0, PLANE, one_block, 0)
-
-        @pl.when(ours)
-        def _():
-            def add_block(t, c):
-                to_sibling(low, t).wait_recv()
-                both = mine[t].astype(jnp.float32) + from_core[low, t].astype(jnp.float32)
-                both = both.astype(jnp.bfloat16)
-
-                @pl.when(t == i)
-                def _():
-                    out_ref[low * PLANE + i] = both
-
-                @pl.when(t != i)
-                def _():
-                    summed[low, t] = both
-                    to_owner(low, t).start()
-
+        lax.fori_loop(0, PLANE - 1, times, 0)
+
+        @pl.when(o >= 1)
+        def _():
+            def plus(n, c):
+                add(n, rows_from(o - 1))
                 return c
 
-            lax.fori_loop(0, PLANE, add_block, 0)
+            lax.fori_loop(0, PLANE - 1, plus, 0)
 
         return carry
 
-    lax.fori_loop(0, PLANE, one_shard, 0)
+    lax.fori_loop(0, PLANE, one_source, 0)
+    for n in range(PLANE - 1):
+        add(jnp.int32(n), rows_from(PLANE - 1))
+
+    take_hop(3)
+
+    def last_shard(o, carry):
+        multiply(jnp.int32(PLANE - 1), rows_from(PLANE - 1 - o))
+
+        @pl.when(o >= 1)
+        def _():
+            add(jnp.int32(PLANE - 1), rows_from(PLANE - o))
+
+        return carry
+
+    lax.fori_loop(0, PLANE, last_shard, 0)
+    add(jnp.int32(PLANE - 1), rows_from(0))
 
     for low in (0, 1):
         for t in range(PLANE):
@@ -426,10 +464,6 @@
                 across_own_sent.wait_send()
         for g in range(kv_heads):
             attn_part(g, o).wait_send()
-    for c in (0, 1):
-        @pl.when(z + 1 < PLANE)
-        def _():
-            up_copy(c).wait_send()
     for k in (1, 2, 3):
         for way in (0, 1):
             @pl.when(sends_hop(way, k))
@@ -457,26 +491,27 @@
     blocks = pl.pallas_call(
         fused_kernel,
         out_shape=jax.ShapeDtypeStruct((2 * PLANE, rows, columns), low),
-        in_specs=[vmem] * 6 + [pl.BlockSpec(memory_space=pltpu.SMEM)],
+        in_specs=[pl.BlockSpec(memory_space=pl.ANY)] * 6 + [pl.BlockSpec(memory_space=pltpu.SMEM)],
         out_specs=vmem,
         scratch_shapes=[
+            pltpu.VMEM((rows, q_cols), low),
             pltpu.VMEM((held, kv_cols), low),
             pltpu.VMEM((held, kv_cols), low),
             pltpu.VMEM((rows, (REACH + 1) * rows), jnp.float32),
             pltpu.VMEM((PLANE, columns, q_cols), low),
             pltpu.VMEM((PLANE, rows, q_cols), low),
-            pltpu.VMEM((PLANE, rows, columns), low),
             pltpu.VMEM((2, PLANE, rows, columns), low),
             pltpu.VMEM((2, PLANE, rows, columns), low),
             pltpu.VMEM((2, PLANE, rows, columns), low),
-            sem((4, 2)), sem((4, 2)), sem((4, 2)), sem((4, 2)),
+            pltpu.VMEM((2, PLANE, rows, columns), low),
+            sem((6,)), sem((4, 2)), sem((4, 2)), sem((4, 2)), sem((4, 2)),
             sem((REACH + 1, 2)), sem((REACH + 1, 2)),
             sem((2, 4)), sem((2, 4)),
             sem((kv_heads, 4)), sem((kv_heads, 4)),
             sem((2, PLANE)), sem((2, PLANE)), sem((2, PLANE)), sem((2, PLANE)),
         ],
         compiler_params=pltpu.CompilerParams(
-            collective_id=0, has_side_effects=True, vmem_limit_bytes=52 * 1024 * 1024
+            collective_id=0, has_side_effects=True, vmem_limit_bytes=60 * 1024 * 1024
         ),
         cost_estimate=pl.CostEstimate(
             flops=12_000_000_000, bytes_accessed=8_000_000, transcendentals=10_000_000

time: 153 us -> 148 us (0.967)
  the two profiles are of different devices: /device:TPU:5 before, /device:TPU:1 now
where the time goes in v3:
time: 148 us; the launch traced here: 147 us
  Pallas kernels  144 us (97%)
  local copies, waits for them, and re-layouts  3.29 us (2%)
    pallas_call x1, Pallas kernels, per_device_fused(): pl.pallas_call(fused_kernel, out_shape=jax.ShapeDtypeStruct((2 * PLANE, r...  144 us

profile of v3, /device:TPU:1, one launch (start us, length us, event | category | flops | bytes accessed | tf_op | source)
XLA Modules:
  0.0 147.4 jit_solution(9658127065936045527)
XLA Ops:
  0.0 144.1 %shard_map.73 = bf16[8,256,320]{2,1,0:T(8,128)(2,1)} custom-call(bf16[256,2560]{1,0:T(8,128)(2,1)} %q_ref.1, bf16[256,512]{1,0:T(8,128)(2,1)} %k_ref.1, bf16[256,512]{1,0:T(8,128)(2,1)} %v_ref.1, bf16[32,512]{1,0:T(8,128)(2,1)} %pk_ref.1, bf16[32,512]{1,0:T(8,128)(2,1)} %pv_ref.1, bf16[320,2560]{1,0:T(8,128)(2,1)} %bitcast.5, s32[16]{0:T(128)} %len_ref.1), custom_call_target="tpu_custom_call" | custom-call | flops 12000000000 | bytes 8000000 | tf_op jit(solution)/shard_map/pallas_call | solution.py:491
  144.1 1.7 %copy.8 = bf16[256,8,320]{0,2,1:T(8,128)(2,1)S(1)} copy(bf16[256,8,320]{2,0,1:T(8,128)(2,1)} %bitcast.4) | data formatting | bytes 2621440 | tf_op jit(solution)/shard_map/transpose | solution.py:523
  145.8 1.6 %copy.9 = bf16[256,2560]{1,0:T(8,128)(2,1)} copy(bf16[256,2560]{0,1:T(8,128)(2,1)S(1)} %bitcast.3) | data formatting | bytes 2621440 | tf_op jit(solution)/shard_map/reshape | solution.py:523

commit v4 on v2

--- a/solution.py
+++ b/solution.py
@@ -294,7 +294,7 @@
                 across_relayed(d, 0).start()
                 across_relayed(d, 1).start()
 
-    for c in range(PIECES):
+    for c in range(PIECES // 2):
         to_far(c).start()
     to_y(0).start()
 
@@ -306,6 +306,8 @@
         def _():
             across_own(d, 0).wait_recv()
             across_own(d, 1).wait_recv()
+    for c in range(PIECES // 2, PIECES):
+        to_far(c).start()
     for c in range(1, PIECES):
         to_y(c).start()
 
@@ -336,11 +338,11 @@
         attn_to_x(g).wait_recv()
         attn_to_near(g).wait_recv()
 
-        @pl.when(lax.rem(g, 2) == 0)
+        @pl.when(g != 1)
         def _():
             near_to_x(g).start()
 
-        @pl.when(lax.rem(g, 2) == 1)
+        @pl.when(g == 1)
         def _():
             x_to_near(g).start()
 
@@ -373,18 +375,19 @@
         def _():
             attn_pass_on(g - 1)
 
+        @pl.when(g == 1)
+        def _():
+            for c in range(PIECES // 2):
+                pass_on(c)
+
         return carry
 
     lax.fori_loop(0, kv_heads, one_group, 0)
     attn_pass_on(jnp.int32(kv_heads - 1))
+    for c in range(PIECES // 2, PIECES):
+        pass_on(c)
     for c in range(PIECES):
-        pass_on(c)
-
-    def take_across(g, carry):
-        near_to_x(g).wait_recv()
-        return carry
-
-    lax.fori_loop(0, kv_heads, take_across, 0)
+        to_y(c).wait_recv()
 
     def to_sibling(low, t):
         return send(to_core.at[low, t], from_core.at[low, t], mp_s.at[low, t], mp_r.at[low, t],
@@ -404,63 +407,88 @@
         return send(summed.at[low, t], out_ref.at[column_block(t, low)], out_s.at[low, t],
                     out_r.at[low, t], member(t))
 
-    def one_shard(n, carry):
+    def shard_of(n):
         hi = z_hi + lax.div(n, 2) * (1 - 2 * z_hi)
         low = y + lax.rem(n, 2) * (1 - 2 * y)
-        src = hi * 2 + low
-        ours = hi == mp
-
-        @pl.when(n == 1)
-        def _():
-            for c in range(PIECES):
-                to_y(c).wait_recv()
-
-        @pl.when(n == 3)
-        def _():
-            for c in range(PIECES):
-                far_to_y(c).wait_recv()
-
-        def one_block(t, c):
-            product = lax.dot_general(
-                attn[t], weights[src], NT, preferred_element_type=jnp.float32
-            ).astype(jnp.bfloat16)
-
-            @pl.when(ours)
+        return hi * 2 + low, low, hi == mp
+
+    def rows_from(o):
+        lo = z_lo + lax.div(o, 2) * (1 - 2 * z_lo)
+        return lo * 2 + x + lax.rem(o, 2) * (1 - 2 * x)
+
+    def multiply(n, t):
+        src, low, ours = shard_of(n)
+        product = lax.dot_general(
+            attn[t], weights[src], NT, preferred_element_type=jnp.float32
+        ).astype(jnp.bfloat16)
+
+        @pl.when(ours)
+        def _():
+            mine[low, t] = product
+
+        @pl.when(jnp.logical_not(ours))
+        def _():
+            to_core[low, t] = product
+            to_sibling(low, t).start()
+
+    def add(n, t):
+        src, low, ours = shard_of(n)
+
+        @pl.when(ours)
+        def _():
+            to_sibling(low, t).wait_recv()
+            both = mine[low, t].astype(jnp.float32) + from_core[low, t].astype(jnp.float32)
+            both = both.astype(jnp.bfloat16)
+
+            @pl.when(t == token)
             def _():
-                mine[t] = product
-
-            @pl.when(jnp.logical_not(ours))
+                out_ref[column_block(token, low)] = both
+
+            @pl.when(t != token)
             def _():
-                to_core[low, t] = product
-                to_sibling(low, t).start()
-
+                summed[low, t] = both
+                to_owner(low, t).start()
+
+    def one_source(o, carry):
+        @pl.when(o == PLANE - 1)
+        def _():
+            for g in range(kv_heads):
+                near_to_x(g).wait_recv()
+
+        def times(n, c):
+            multiply(n, rows_from(o))
             return c
 
-        lax.fori_loop(0, PLANE, one_block, 0)
-
-        @pl.when(ours)
-        def _():
-            def add_block(t, c):
-                to_sibling(low, t).wait_recv()
-                both = mine[t].astype(jnp.float32) + from_core[low, t].astype(jnp.float32)
-                both = both.astype(jnp.bfloat16)
-
-                @pl.when(t == token)
-                def _():
-                    out_ref[column_block(token, low)] = both
-
-                @pl.when(t != token)
-                def _():
-                    summed[low, t] = both
-                    to_owner(low, t).start()
-
+        lax.fori_loop(0, PLANE - 1, times, 0)
+
+        @pl.when(o >= 1)
+        def _():
+            def plus(n, c):
+                add(n, rows_from(o - 1))
                 return c
 
-            lax.fori_loop(0, PLANE, add_block, 0)
+            lax.fori_loop(0, PLANE - 1, plus, 0)
 
         return carry
 
-    lax.fori_loop(0, PLANE, one_shard, 0)
+    lax.fori_loop(0, PLANE, one_source, 0)
+    for n in range(PLANE - 1):
+        add(jnp.int32(n), rows_from(PLANE - 1))
+
+    for c in range(PIECES):
+        far_to_y(c).wait_recv()
+
+    def last_shard(o, carry):
+        multiply(jnp.int32(PLANE - 1), rows_from(PLANE - 1 - o))
+
+        @pl.when(o >= 1)
+        def _():
+            add(jnp.int32(PLANE - 1), rows_from(PLANE - o))
+
+        return carry
+
+    lax.fori_loop(0, PLANE, last_shard, 0)
+    add(jnp.int32(PLANE - 1), rows_from(0))
 
     for low in (0, 1):
         for t in range(PLANE):
@@ -523,7 +551,7 @@
             pltpu.VMEM((rows, (REACH + 1) * rows), jnp.float32),
             pltpu.VMEM((PLANE, columns, q_cols), low),
             pltpu.VMEM((PLANE, rows, q_cols), low),
-            pltpu.VMEM((PLANE, rows, columns), low),
+            pltpu.VMEM((2, PLANE, rows, columns), low),
             pltpu.VMEM((2, PLANE, rows, columns), low),
             pltpu.VMEM((2, PLANE, rows, columns), low),
             pltpu.VMEM((2, PLANE, rows, columns), low),

time: 176 us -> 158 us (0.90)
  Pallas kernels: 171 us -> 152 us
    pallas_call x1, Pallas kernels: 171 us -> 152 us  [per_device_fused(): pl.pallas_call(fused_kernel, out_shape=jax.ShapeDtypeStruct((2 * PLANE, r...]
where the time goes in v4:
time: 158 us; the launch traced here: 155 us
  Pallas kernels  152 us (96%)
  local copies, waits for them, and re-layouts  3.29 us (2%)
    pallas_call x1, Pallas kernels, per_device_fused(): pl.pallas_call(fused_kernel, out_shape=jax.ShapeDtypeStruct((2 * PLANE, r...  152 us

profile of v4, /device:TPU:5, one launch (start us, length us, event | category | flops | bytes accessed | tf_op | source)
XLA Modules:
  0.0 155.5 jit_solution(17918309544415012331)
XLA Ops:
  0.0 152.2 %shard_map.73 = bf16[8,256,320]{2,1,0:T(8,128)(2,1)} custom-call(bf16[256,2560]{1,0:T(8,128)(2,1)} %q_ref.1, bf16[256,512]{1,0:T(8,128)(2,1)} %k_ref.1, bf16[256,512]{1,0:T(8,128)(2,1)} %v_ref.1, bf16[32,512]{1,0:T(8,128)(2,1)} %pk_ref.1, bf16[32,512]{1,0:T(8,128)(2,1)} %pv_ref.1, bf16[320,2560]{1,0:T(8,128)(2,1)} %bitcast.5, s32[16]{0:T(128)} %len_ref.1), custom_call_target="tpu_custom_call" | custom-call | flops 12000000000 | bytes 8000000 | tf_op jit(solution)/shard_map/pallas_call | solution.py:542
  152.2 1.7 %copy.8 = bf16[256,8,320]{0,2,1:T(8,128)(2,1)S(1)} copy(bf16[256,8,320]{2,0,1:T(8,128)(2,1)} %bitcast.4) | data formatting | bytes 2621440 | tf_op jit(solution)/shard_map/transpose | solution.py:574
  153.9 1.6 %copy.9 = bf16[256,2560]{1,0:T(8,128)(2,1)} copy(bf16[256,2560]{0,1:T(8,128)(2,1)S(1)} %bitcast.3) | data formatting | bytes 2621440 | tf_op jit(solution)/shard_map/reshape | solution.py:574

commit v5 on v3

--- a/solution.py
+++ b/solution.py
@@ -143,6 +143,11 @@
     mp = lax.axis_index("mp")
     z = lax.div(me, PLANE)
     i = lax.rem(me, PLANE)
+    y, x = lax.div(i, 2), lax.rem(i, 2)
+    x_mate = me + 1 - 2 * x
+    y_mate = me + 2 * (1 - 2 * y)
+    x_token = i + 1 - 2 * x
+    y_token = i + 2 * (1 - 2 * y)
 
     def send(src, dst, send_sem, recv_sem, blk, core=None):
         return pltpu.make_async_remote_copy(
@@ -307,10 +312,37 @@
     exponent_scale = math.log2(math.e) / math.sqrt(HEAD_SIZE)
     width = group * HEAD_SIZE
 
-    def attn_part(g, o):
+    def attn_block(t, g):
         columns = pl.ds(pl.multiple_of(g * width, HEAD_SIZE), width)
-        block = attn.at[i, :, columns]
-        return send(block, block, at_s.at[g, o], at_r.at[g, o], in_plane(o))
+        return attn.at[t, :, columns]
+
+    def attn_to_x(g):
+        block = attn_block(i, g)
+        return send(block, block, at_s.at[g, 0], at_r.at[g, 0], x_mate)
+
+    def attn_to_y(g):
+        block = attn_block(i, g)
+        return send(block, block, at_s.at[g, 1], at_r.at[g, 1], y_mate)
+
+    def y_to_x(g):
+        block = attn_block(y_token, g)
+        return send(block, block, at_s.at[g, 2], at_r.at[g, 2], x_mate)
+
+    def x_to_y(g):
+        block = attn_block(x_token, g)
+        return send(block, block, at_s.at[g, 2], at_r.at[g, 2], y_mate)
+
+    def attn_pass_on(g):
+        attn_to_x(g).wait_recv()
+        attn_to_y(g).wait_recv()
+
+        @pl.when(lax.rem(g, 2) == 0)
+        def _():
+            y_to_x(g).start()
+
+        @pl.when(lax.rem(g, 2) == 1)
+        def _():
+            x_to_y(g).start()
 
     def one_group(g, carry):
         head = pl.ds(pl.multiple_of(g * HEAD_SIZE, HEAD_SIZE), HEAD_SIZE)
@@ -334,20 +366,25 @@
                 preferred_element_type=jnp.float32,
             )
             attn[i, :, column] = (mixed / total).astype(jnp.bfloat16)
-        for o in (1, 2, 3):
-            attn_part(g, o).start()
-
-        @pl.when(g == 1)
+        attn_to_x(g).start()
+        attn_to_y(g).start()
+
+        @pl.when(g == 0)
         def _():
             take_hop(1)
             start_hop(2)
 
+        @pl.when(g >= 1)
+        def _():
+            attn_pass_on(g - 1)
+
         return carry
 
     lax.fori_loop(0, kv_heads, one_group, 0)
 
     take_hop(2)
     start_hop(3)
+    attn_pass_on(jnp.int32(kv_heads - 1))
 
     def to_sibling(low, t):
         return send(to_core.at[low, t], from_core.at[low, t], mp_s.at[low, t], mp_r.at[low, t],
@@ -368,7 +405,7 @@
         return src, lax.rem(src, 2), lax.div(src, 2) == mp
 
     def rows_from(o):
-        return lax.rem(i - o + PLANE, PLANE)
+        return (y + lax.div(o, 2) * (1 - 2 * y)) * 2 + x + lax.rem(o, 2) * (1 - 2 * x)
 
     def multiply(n, t):
         src, low, ours = shard(n)
@@ -404,11 +441,10 @@
                 to_owner(low, t).start()
 
     def one_source(o, carry):
-        for v in (1, 2, 3):
-            @pl.when(o == v)
-            def _():
-                for g in range(kv_heads):
-                    attn_part(g, v).wait_recv()
+        @pl.when(o == PLANE - 1)
+        def _():
+            for g in range(kv_heads):
+                y_to_x(g).wait_recv()
 
         def times(n, c):
             multiply(n, rows_from(o))
@@ -462,8 +498,10 @@
             @pl.when((i + o < PLANE) | (z >= 1))
             def _():
                 across_own_sent.wait_send()
-        for g in range(kv_heads):
-            attn_part(g, o).wait_send()
+    for g in range(kv_heads):
+        attn_to_x(g).wait_send()
+        attn_to_y(g).wait_send()
+        y_to_x(g).wait_send()
     for k in (1, 2, 3):
         for way in (0, 1):
             @pl.when(sends_hop(way, k))
@@ -507,7 +545,7 @@
             sem((6,)), sem((4, 2)), sem((4, 2)), sem((4, 2)), sem((4, 2)),
             sem((REACH + 1, 2)), sem((REACH + 1, 2)),
             sem((2, 4)), sem((2, 4)),
-            sem((kv_heads, 4)), sem((kv_heads, 4)),
+            sem((kv_heads, 3)), sem((kv_heads, 3)),
             sem((2, PLANE)), sem((2, PLANE)), sem((2, PLANE)), sem((2, PLANE)),
         ],
         compiler_params=pltpu.CompilerParams(

time: 148 us -> 146 us (0.986)
  the two profiles are of different devices: /device:TPU:1 before, /device:TPU:5 now
where the time goes in v5:
time: 146 us; the launch traced here: 144 us
  Pallas kernels  140 us (96%)
  local copies, waits for them, and re-layouts  3.29 us (2%)
    pallas_call x1, Pallas kernels, per_device_fused(): pl.pallas_call(fused_kernel, out_shape=jax.ShapeDtypeStruct((2 * PLANE, r...  140 us

profile of v5, /device:TPU:5, one launch (start us, length us, event | category | flops | bytes accessed | tf_op | source)
XLA Modules:
  0.0 143.8 jit_solution(14717015608193207761)
XLA Ops:
  0.0 140.4 %shard_map.73 = bf16[8,256,320]{2,1,0:T(8,128)(2,1)} custom-call(bf16[256,2560]{1,0:T(8,128)(2,1)} %q_ref.1, bf16[256,512]{1,0:T(8,128)(2,1)} %k_ref.1, bf16[256,512]{1,0:T(8,128)(2,1)} %v_ref.1, bf16[32,512]{1,0:T(8,128)(2,1)} %pk_ref.1, bf16[32,512]{1,0:T(8,128)(2,1)} %pv_ref.1, bf16[320,2560]{1,0:T(8,128)(2,1)} %bitcast.5, s32[16]{0:T(128)} %len_ref.1), custom_call_target="tpu_custom_call" | custom-call | flops 12000000000 | bytes 8000000 | tf_op jit(solution)/shard_map/pallas_call | solution.py:529
  140.5 1.7 %copy.8 = bf16[256,8,320]{0,2,1:T(8,128)(2,1)S(1)} copy(bf16[256,8,320]{2,0,1:T(8,128)(2,1)} %bitcast.4) | data formatting | bytes 2621440 | tf_op jit(solution)/shard_map/transpose | solution.py:561
  142.2 1.6 %copy.9 = bf16[256,2560]{1,0:T(8,128)(2,1)} copy(bf16[256,2560]{0,1:T(8,128)(2,1)S(1)} %bitcast.3) | data formatting | bytes 2621440 | tf_op jit(solution)/shard_map/reshape | solution.py:561

commit v6 on v5

--- a/solution.py
+++ b/solution.py
@@ -468,17 +468,27 @@
 
     take_hop(3)
 
-    def last_shard(o, carry):
-        multiply(jnp.int32(PLANE - 1), rows_from(PLANE - 1 - o))
-
-        @pl.when(o >= 1)
-        def _():
-            add(jnp.int32(PLANE - 1), rows_from(PLANE - o))
-
+    src, low, ours = shard(jnp.int32(PLANE - 1))
+    product = lax.dot_general(
+        attn[...].reshape(PLANE * rows, attn.shape[2]), weights[src], NT,
+        preferred_element_type=jnp.float32,
+    ).astype(jnp.bfloat16).reshape(PLANE, rows, w_ref.shape[0])
+
+    @pl.when(ours)
+    def _():
+        mine[low] = product
+
+    @pl.when(jnp.logical_not(ours))
+    def _():
+        to_core[low] = product
+        for t in range(PLANE):
+            to_sibling(low, t).start()
+
+    def last_sum(o, carry):
+        add(jnp.int32(PLANE - 1), rows_from(PLANE - 1 - o))
         return carry
 
-    lax.fori_loop(0, PLANE, last_shard, 0)
-    add(jnp.int32(PLANE - 1), rows_from(0))
+    lax.fori_loop(0, PLANE, last_sum, 0)
 
     for low in (0, 1):
         for t in range(PLANE):

time: 146 us -> 147 us (level)
  Pallas kernels: 140 us -> 143 us
    pallas_call x1, Pallas kernels: 140 us -> 143 us  [per_device_fused(): pl.pallas_call(fused_kernel, out_shape=jax.ShapeDtypeStruct((2 * PLANE, r...]
where the time goes in v6:
time: 147 us; the launch traced here: 146 us
  Pallas kernels  143 us (97%)
  local copies, waits for them, and re-layouts  3.29 us (2%)
    pallas_call x1, Pallas kernels, per_device_fused(): pl.pallas_call(fused_kernel, out_shape=jax.ShapeDtypeStruct((2 * PLANE, r...  143 us

profile of v6, /device:TPU:5, one launch (start us, length us, event | category | flops | bytes accessed | tf_op | source)
XLA Modules:
  0.0 145.8 jit_solution(899453205395370177)
XLA Ops:
  0.0 142.5 %shard_map.73 = bf16[8,256,320]{2,1,0:T(8,128)(2,1)} custom-call(bf16[256,2560]{1,0:T(8,128)(2,1)} %q_ref.1, bf16[256,512]{1,0:T(8,128)(2,1)} %k_ref.1, bf16[256,512]{1,0:T(8,128)(2,1)} %v_ref.1, bf16[32,512]{1,0:T(8,128)(2,1)} %pk_ref.1, bf16[32,512]{1,0:T(8,128)(2,1)} %pv_ref.1, bf16[320,2560]{1,0:T(8,128)(2,1)} %bitcast.5, s32[16]{0:T(128)} %len_ref.1), custom_call_target="tpu_custom_call" | custom-call | flops 12000000000 | bytes 8000000 | tf_op jit(solution)/shard_map/pallas_call | solution.py:539
  142.5 1.7 %copy.8 = bf16[256,8,320]{0,2,1:T(8,128)(2,1)S(1)} copy(bf16[256,8,320]{2,0,1:T(8,128)(2,1)} %bitcast.4) | data formatting | bytes 2621440 | tf_op jit(solution)/shard_map/transpose | solution.py:571
  144.3 1.6 %copy.9 = bf16[256,2560]{1,0:T(8,128)(2,1)} copy(bf16[256,2560]{0,1:T(8,128)(2,1)S(1)} %bitcast.3) | data formatting | bytes 2621440 | tf_op jit(solution)/shard_map/reshape | solution.py:571
